TPU v7x, 256 devices: a whole 4x4x8 slice. The times are simulated.
256 devices in a mesh: shot: 32 (over z, y_hi, core), rcv: 8 (over x, y_lo).
Axes of the slice: x: 4, y: 4 (y_hi: 2, y_lo: 2; y = y_hi * 2 + y_lo), z: 8, core: 2. Of those that a mesh axis runs over, the one named last changes fastest.
Arguments:
- left_traces: float32 [32, 4096, 2048], P('shot', 'rcv'), may hold values from -6 to 6
- right_traces: float32 [4096, 64, 2048], P('shot', 'rcv'), may hold values from -6 to 6
Outputs:
- multiples: float32 [32, 64, 2048], P('shot', 'rcv')
All inputs are finite; a program needn't handle non-finite values.
Results may differ from a plain program's by a relative error of at most 0.0041.
Values may be sent and summed in bfloat16 or wider, within the bound.
No kernel may reach another device: no remote copies, remote signals or barrier semaphores. Data moves between devices by JAX's collectives and lax.ppermute only.
A program may use at most 320 MiB of HBM per device.

v0:
```python
import math

import jax
import jax.numpy as jnp
from jax import lax
from jax.sharding import PartitionSpec as P

K = 4096
NF = 128
F_LO = 256


def frequency_table(first_bin, bin_count, sample_count):
    bin_index = first_bin + lax.iota(jnp.int32, bin_count)
    time_index = lax.iota(jnp.int32, sample_count)
    phase_int = bin_index[:, None] * time_index[None, :] % sample_count
    radians = phase_int.astype(jnp.float32) * (2.0 * math.pi / sample_count)
    return jnp.concatenate([jnp.cos(radians), -jnp.sin(radians)], 0)


def complex_terms(left_part, right_part):
    half_count = left_part.shape[0] // 2
    col_count = right_part.shape[1]
    left_complex_pair = jnp.concatenate([left_part[:half_count], left_part[half_count:]], 2)
    right_real_component = jnp.concatenate([right_part[:half_count], -right_part[half_count:]], 2)
    right_imaginary = jnp.concatenate([right_part[half_count:], right_part[:half_count]], 2)
    right_complex_pair = jnp.concatenate([right_real_component, right_imaginary], 1)
    complex_product = jnp.einsum(
        "zhn,zqn->zhq", left_complex_pair, right_complex_pair, preferred_element_type=jnp.float32
    )
    return jnp.concatenate(
        [complex_product[:, :, :col_count], complex_product[:, :, col_count:]], 0
    )


def batch_output(left_traces, right_traces, first_bin, bin_count):
    exact_arithmetic = lax.Precision.HIGHEST
    sample_count = left_traces.shape[2]
    freq_table = frequency_table(first_bin, bin_count, sample_count)
    forward_table = freq_table * (1.0 / math.sqrt(sample_count))
    left_spec = jnp.einsum(
        "ct,skt->csk",
        forward_table,
        left_traces,
        precision=exact_arithmetic,
        preferred_element_type=jnp.float32,
    ).astype(jnp.bfloat16)
    right_spec = jnp.einsum(
        "ct,krt->crk",
        forward_table,
        right_traces,
        precision=exact_arithmetic,
        preferred_element_type=jnp.float32,
    ).astype(jnp.bfloat16)
    left_all = lax.all_gather(left_spec, "rcv", axis=2, tiled=True)
    summed = complex_terms(left_all, lax.all_gather(right_spec, "shot", axis=2, tiled=True))
    spectrum = summed * (1.0 / math.sqrt(K))
    return jnp.einsum("csr,ct->srt", spectrum, freq_table, precision=exact_arithmetic) * math.sqrt(
        2.0 / NF
    )


def shards(left_traces, right_traces):
    multiples = batch_output(left_traces, right_traces, F_LO, NF)
    return multiples


def solution(mesh):
    placed = (P("shot", "rcv", None), P("shot", "rcv", None))
    return jax.shard_map(
        shards, mesh=mesh, in_specs=placed, out_specs=P("shot", "rcv", None), check_vma=False
    )
```

profile of v0, /device:TPU:1, one launch (start us, length us, event | category | flops | bytes accessed | tf_op | source)
XLA Modules:
  0.0 310.3 jit_solution(6636638617706694164)
XLA Ops:
  6.5 0.0 all-gather.6.cloned.1.call-start
  6.5 4.2 %fusion.34 = (f32[128,2048]{1,0:T(8,128)S(1)}, f32[128,2048]{1,0:T(8,128)S(1)}) fusion(s32[128]{0:T(128)S(1)} %iota_add_fusion), kind=kLoop, calls=%fused_computation.32 | loop fusion | flops 3932160 | bytes 2097664 | tf_op jit(solution)/shard_map/cos | solution.py:18
  10.7 6.6 %fusion.21 = bf16[256,512]{1,0:T(8,128)(2,1)} fusion(f32[1,512,2048]{2,1,0:T(8,128)} %param.2, f32[128,2048]{1,0:T(8,128)S(1)} %get-tuple-element.13, f32[128,2048]{1,0:T(8,128)S(1)} %get-tuple-element.12), kind=kOutput, calls=%fused_computation.20 | convolution fusion | flops 3222405120 | bytes 6553600 | tf_op jit(solution)/shard_map/ct,skt->csk/dot_general | solution.py:41
  17.3 0.0 all-gather.6.cloned.1.call-update
  17.4 0.2 all-gather.4.cloned.1.call-start
  17.6 16.0 %fusion.16 = bf16[256,8,128]{2,0,1:T(8,128)(2,1)} fusion(f32[128,8,2048]{2,1,0:T(8,128)} %param.3, f32[128,2048]{1,0:T(8,128)S(1)} %get-tuple-element.13, f32[128,2048]{1,0:T(8,128)S(1)} %get-tuple-element.12), kind=kOutput, calls=%fused_computation.19 | convolution fusion | flops 6443761664 | bytes 11010048 | tf_op jit(solution)/shard_map/ct,krt->crk/dot_general | solution.py:48
  33.6 0.0 all-gather.4.cloned.1.call-update
  33.6 40.8 %all-gather.6.cloned.1.call-done = bf16[256,4096]{1,0:T(8,128)(2,1)} async-done(((bf16[256,512]{1,0:T(8,128)(2,1)}), bf16[256,4096]{1,0:T(8,128)(2,1)}) %all-gather.6.cloned.1.call-update) | async-done | bytes 2097168 | tf_op jit(solution)/shard_map/all_gather | solution.py:55
  74.4 1.7 slice_bitcast_fusion.1
  76.2 1.5 maximum_bitcast_fusion
  77.7 153.3 %all-gather.4.cloned.1.call-done = bf16[256,8,4096]{2,0,1:T(8,128)(2,1)} async-done(((bf16[256,8,128]{2,0,1:T(8,128)(2,1)}), bf16[256,8,4096]{2,0,1:T(8,128)(2,1)}) %all-gather.4.cloned.1.call-update) | async-done | bytes 16777232 | tf_op jit(solution)/shard_map/all_gather | solution.py:56
  231.0 15.0 %slice_negate_fusion = (bf16[128,8,4096]{2,0,1:T(8,128)(2,1)}, bf16[128,8,4096]{2,0,1:T(8,128)(2,1)}, bf16[128,8,4096]{2,0,1:T(8,128)(2,1)}) fusion(bf16[256,8,4096]{2,0,1:T(8,128)(2,1)} %all-gather.4.cloned.1.call-done), kind=kLoop, calls=%fused_computation.44 | loop fusion | flops 4194304 | bytes 41943040 | tf_op jit(solution)/shard_map/neg | solution.py:25
  246.0 0.0 copy-start
  246.0 23.2 %maximum_maximum_fusion = bf16[128,16,8192]{2,0,1:T(8,128)(2,1)} fusion(bf16[128,8,4096]{2,0,1:T(8,128)(2,1)} %get-tuple-element.7, bf16[128,8,4096]{2,0,1:T(8,128)(2,1)} %get-tuple-element.6, bf16[128,8,4096]{2,0,1:T(8,128)(2,1)} %get-tuple-element.5), kind=kLoop, calls=%fused_computation | loop fusion | flops 134217728 | bytes 58720256 | tf_op jit(solution)/shard_map/concatenate | solution.py:27
  269.2 0.0 copy-done
  269.2 32.1 %fusion = f32[128,1,16]{2,1,0:T(1,128)S(1)} fusion(bf16[128,16,8192]{2,0,1:T(8,128)(2,1)} %maximum_maximum_fusion, bf16[128,8192,1]{1,0,2:T(8,128)(2,1)S(1)} %copy-done), kind=kOutput, calls=%fused_computation.1 | convolution fusion | flops 33554432 | bytes 35659776 | tf_op jit(solution)/shard_map/zhn,zqn->zhq/dot_general | solution.py:28
  301.4 0.2 fusion.44
  301.6 0.1 copy.9
  301.7 1.8 fusion.7
  (2 shorter events, 0.1 us)
Async XLA Ops:
  6.5 67.9 %all-gather.6.cloned.1.call-start = ((), (), s32[]{:S(2)}) async-start(), calls=%async_computation.1 | async-start | bytes 2359296 | tf_op jit(solution)/shard_map/all_gather | solution.py:55
  17.4 213.6 %all-gather.4.cloned.1.call-start = ((), (), s32[]{:S(2)}) async-start(), calls=%async_computation | async-start | bytes 17301504 | tf_op jit(solution)/shard_map/all_gather | solution.py:56
  246.0 23.2 %copy-start = (bf16[128,8192,1]{1,0,2:T(8,128)(2,1)S(1)}, bf16[128,8192,1]{1,0,2:T(8,128)(2,1)}, u32[]{:S(2)}) copy-start(bf16[128,8192,1]{1,0,2:T(8,128)(2,1)} %maximum_bitcast_fusion) | copy-start | bytes 6291460
Sparse Core Ops, SparseCore 0:
  17.5 56.8 all-gather.5
  77.0 153.9 all-gather.3
where the time goes:
time: 310 us
  waiting for transfers between devices  194 us (63%)
  matrix products  56.5 us (18%)
  other arithmetic  43.9 us (14%)
  between operations  13.4 us (4%)
    all_gather x1, waiting for transfers between devices, batch_output(): lax.all_gather(right_spec, 'shot', axis=2, tiled=True)  153 us
    all_gather x1, waiting for transfers between devices, batch_output(): left_all = lax.all_gather(left_spec, 'rcv', axis=2, tiled=True)  40.8 us
    dot_general x1, matrix products, complex_terms(): jnp.einsum('zhn,zqn->zhq', left_complex_pair, right_complex_pair, preferr...  32.1 us
    concatenate x1, other arithmetic, complex_terms(): jnp.concatenate([right_real_component, right_imaginary], 1)  23.2 us
    dot_general x1, matrix products, batch_output(): jnp.einsum('ct,krt->crk', forward_table, right_traces, precision=exact_ar...  16 us
    neg x1, other arithmetic, complex_terms(): -right_part[half_count:]  15 us
    dot_general x1, matrix products, batch_output(): jnp.einsum('ct,skt->csk', forward_table, left_traces, precision=exact_ari...  6.63 us
  transfers between devices with their start and end apart: 2, of which 2 were waited for; matrix products, arithmetic and copies ran while one was open for 6% of the time, Pallas kernels for 0%

commit v1 on v0

v1 whole, which is shorter than its diff:
```python
import math

import jax
import jax.numpy as jnp
import ml_dtypes
import numpy as np
from jax import lax
from jax.experimental import pallas as pl
from jax.experimental.pallas import tpu as pltpu
from jax.sharding import Mesh, PartitionSpec as P

K = 4096
NT = 2048
NF = 128
F_LO = 256
HALF = NT // 2
TB = 256
ALL = ("z", "yh", "core", "x", "yl")
PLANE = ("x", "yl", "yh", "core")


def bins_of_plane():
    even = F_LO + 2 * np.arange(NF // 2)
    return np.concatenate([even, even + 1]).reshape(32, 4)


def table_rows(bins):
    phase = (bins[..., None] * np.arange(NT)) % NT * (2.0 * np.pi / NT)
    return np.stack([np.cos(phase), -np.sin(phase)], -2)


def split_bf16(x):
    hi = x.astype(np.float32).astype(ml_dtypes.bfloat16)
    lo = (x - hi.astype(np.float64)).astype(np.float32).astype(ml_dtypes.bfloat16)
    return hi, lo


def dft_kernel(te_ref, to_ref, la_ref, lb_ref, ra0_ref, ra1_ref, rb0_ref, rb1_ref, out_ref, acc_ref):
    step = pl.program_id(0)
    nt = (((1,), (1,)), ((), ()))

    @pl.when(step == 0)
    def _():
        acc_ref[...] = jnp.zeros_like(acc_ref)

    for blk in range(6):
        if blk < 2:
            rows = pl.ds(blk * 256, 256)
            a, b = la_ref[rows, :], lb_ref[rows, :]
        else:
            r0 = 2 * (blk - 2)
            a, b = (
                jnp.concatenate(
                    [
                        jnp.concatenate([ref[pl.ds(r0 + n, 128, stride=8), :] for ref in refs], 1)
                        for n in range(2)
                    ],
                    0,
                )
                for refs in ((ra0_ref, ra1_ref), (rb0_ref, rb1_ref))
            )
        for half, t_ref in enumerate((te_ref, to_ref)):
            x = a - b if half else a + b
            hi = x.astype(jnp.bfloat16)
            lo = (x - hi.astype(jnp.float32)).astype(jnp.bfloat16)
            y = lax.dot_general(t_ref[...], hi, nt, preferred_element_type=jnp.float32)
            w = lax.dot_general(t_ref[:128, :], lo, nt, preferred_element_type=jnp.float32)
            acc_ref[half * 128 : half * 128 + 128, blk * 256 : blk * 256 + 256] += y[:128] + (y[128:] + w)

    @pl.when(step == pl.num_programs(0) - 1)
    def _():
        for blk in range(6):
            v = acc_ref[:, blk * 256 : blk * 256 + 256] * (1.0 / math.sqrt(NT))
            pair = [v[:, n * 128 : n * 128 + 128].reshape(32, 8, 128) for n in range(2)]
            out_ref[:, blk * 16 : blk * 16 + 16, :] = jnp.concatenate(pair, 1).astype(jnp.bfloat16)


def spectra(left, right, te, to):
    steps = HALF // TB
    lo_half, hi_half = (lambda i: (0, i)), (lambda i: (0, i + steps))
    return pl.pallas_call(
        dft_kernel,
        grid=(steps,),
        out_shape=jax.ShapeDtypeStruct((32, 96, 128), jnp.bfloat16),
        in_specs=[
            pl.BlockSpec((256, TB), lo_half),
            pl.BlockSpec((256, TB), lo_half),
            pl.BlockSpec((512, TB), lo_half),
            pl.BlockSpec((512, TB), hi_half),
            pl.BlockSpec((1024, 128), lambda i: (0, 2 * i)),
            pl.BlockSpec((1024, 128), lambda i: (0, 2 * i + 1)),
            pl.BlockSpec((1024, 128), lambda i: (0, 2 * (i + steps))),
            pl.BlockSpec((1024, 128), lambda i: (0, 2 * (i + steps) + 1)),
        ],
        out_specs=pl.BlockSpec((32, 96, 128), lambda i: (0, 0, 0)),
        scratch_shapes=[pltpu.VMEM((256, 1536), jnp.float32)],
        compiler_params=pltpu.CompilerParams(
            dimension_semantics=("arbitrary",), vmem_limit_bytes=40 * 2**20
        ),
        name="spectra",
    )(te, to, left, left, right, right, right, right)


def product_kernel(l_ref, g_ref, out_ref, lf_ref, rf_ref):
    lf_ref[...] = l_ref[...].astype(jnp.float32)
    for p in range(32):
        rf_ref[p * 64 : p * 64 + 64, :] = g_ref[p * 96 + 32 : p * 96 + 96, :].astype(jnp.float32)
    outs = []
    for f in range(4):
        left = [lf_ref[pl.ds(q * 8 + 2 * f + ri, 32, stride=32), :] for ri in range(2) for q in range(4)]
        lhs = jnp.concatenate(left, 1).astype(jnp.bfloat16)
        real_rows, imag_rows = [], []
        for yc in range(4):
            top, bottom = [], []
            for j in range(8):
                base = (j * 4 + yc) * 64 + 2 * f
                re = rf_ref[pl.ds(base, 8, stride=8), :]
                im = rf_ref[pl.ds(base + 1, 8, stride=8), :]
                top += [re, im]
                bottom += [-im, re]
            real_rows.append(jnp.concatenate(top, 0))
            imag_rows.append(jnp.concatenate(bottom, 0))
        rhs = jnp.concatenate(real_rows + imag_rows, 1).astype(jnp.bfloat16)
        outs.append(
            lax.dot_general(lhs, rhs, (((1,), (1,)), ((), ())), preferred_element_type=jnp.float32)
        )
    group = lax.broadcasted_iota(jnp.int32, (32, 128), 1) // 16
    for j in range(8):
        v = jnp.zeros((32, 128), jnp.float32)
        for f in range(4):
            moved = outs[f] if f == j else pltpu.roll(outs[f], (f - j) * 16 % 128, 1)
            v = jnp.where(group == f, moved, v)
        out_ref[pl.ds(j, 32, stride=8), :] = v


def product(left, gathered):
    return pl.pallas_call(
        product_kernel,
        out_shape=jax.ShapeDtypeStruct((256, 128), jnp.float32),
        scratch_shapes=[pltpu.VMEM((1024, 128), jnp.float32), pltpu.VMEM((2048, 128), jnp.float32)],
        compiler_params=pltpu.CompilerParams(vmem_limit_bytes=32 * 2**20),
        name="product",
    )(left, gathered)


def shards(left_traces, right_traces):
    table = table_rows(bins_of_plane())
    forward = table[..., :HALF].reshape(2, 128, HALF)
    te, to = (np.concatenate(split_bf16(forward[n]), 0) for n in range(2))
    sent = spectra(left_traces.reshape(512, NT), right_traces.reshape(1024, NT), te, to)
    here = lax.all_to_all(sent, PLANE, 0, 0, tiled=True)
    left = lax.all_to_all(here[:, :32, :].reshape(8, 128, 128), "z", 0, 0, tiled=True)
    part = product(left.reshape(1024, 128), here.reshape(3072, 128))
    parts = lax.all_to_all(part, ALL, 0, 0, tiled=True)
    spectrum = parts.reshape(8, 32, 128)[:, :, :64].sum(0).reshape(256, 8)
    inverse = table.reshape(8, 4, 8, NT).transpose(1, 0, 2, 3).reshape(256, NT).astype(np.float32)
    out = lax.dot_general(
        spectrum, inverse, (((0,), (0,)), ((), ())), precision=lax.Precision.HIGHEST
    ) * (math.sqrt(2.0 / NF) / math.sqrt(K))
    return out.reshape(1, 8, NT)


def solution(mesh):
    finer = Mesh(mesh.devices.reshape(8, 2, 2, 4, 2), ALL)
    placed = P(("z", "yh", "core"), ("x", "yl"), None)
    return jax.shard_map(
        shards, mesh=finer, in_specs=(placed, placed), out_specs=placed, check_vma=False
    )
```

time: 310 us -> 79.8 us (0.26)
  waiting for transfers between devices: 194 us -> 0 us
  blocking collectives: 0 us -> 61.3 us
  matrix products: 56.5 us -> 1.74 us
  other arithmetic: 43.9 us -> 0.01 us
  between operations: 13.4 us -> 0.05 us
  Pallas kernels: 0 us -> 8.53 us
  local copies, waits for them, and re-layouts: 2.07 us -> 7.77 us
    all_gather x2 -> x0, waiting for transfers between devices: 194 us -> none  [the longest x1 153 us: batch_output(): lax.all_gather(right_spec, 'shot', axis=2, tiled=True)]
    all_to_all x0 -> x3, blocking collectives: none -> 61.3 us  [the longest x1 22.5 us: shards(): here = lax.all_to_all(sent, PLANE, 0, 0, tiled=True)]
    dot_general x4 -> x1, matrix products: 56.5 us -> 1.74 us  [shards(): lax.dot_general(spectrum, inverse, (((0,), (0,)), ((), ())), precision=la...]
    concatenate x1 -> x0, other arithmetic: 23.2 us -> none  [complex_terms(): jnp.concatenate([right_real_component, right_imaginary], 1)]
    neg x1 -> x0, other arithmetic: 15 us -> none  [complex_terms(): -right_part[half_count:]]
    pallas_call x0 -> x2, Pallas kernels: none -> 8.53 us  [the longest x1 7.73 us: spectra(): pl.pallas_call(dft_kernel, grid=(steps,), out_shape=jax.ShapeDtypeStruct(...]
    unnamed x4 -> x10, local copies, waits for them, and re-layouts: 0.12 us -> 7.66 us
    cos x1 -> x0, other arithmetic: 4.16 us -> none  [frequency_table(): return jnp.concatenate([jnp.cos(radians), -jnp.sin(radians)], 0)]
  transfers between devices with their start and end apart: 2 -> 0, of which waited for: 2 -> 0; matrix products, arithmetic and copies ran while one was open for 6% -> 0% of each run, Pallas kernels for 0% -> 0%
where the time goes in v1:
time: 79.8 us; the launch traced here: 79.4 us
  blocking collectives  61.3 us (77%)
  Pallas kernels  8.53 us (11%)
  local copies, waits for them, and re-layouts  7.77 us (10%)
  matrix products  1.74 us (2%)
    all_to_all x1, blocking collectives, shards(): here = lax.all_to_all(sent, PLANE, 0, 0, tiled=True)  22.5 us
    all_to_all x1, blocking collectives, shards(): lax.all_to_all(here[:, :32, :].reshape(8, 128, 128), 'z', 0, 0, tiled=True)  20.3 us
    all_to_all x1, blocking collectives, shards(): parts = lax.all_to_all(part, ALL, 0, 0, tiled=True)  18.5 us
    pallas_call x1, Pallas kernels, spectra(): pl.pallas_call(dft_kernel, grid=(steps,), out_shape=jax.ShapeDtypeStruct(...  7.73 us
    unnamed x10, local copies, waits for them, and re-layouts  7.66 us
    dot_general x1, matrix products, shards(): lax.dot_general(spectrum, inverse, (((0,), (0,)), ((), ())), precision=la...  1.74 us

profile of v1, /device:TPU:1, one launch (start us, length us, event | category | flops | bytes accessed | tf_op | source)
XLA Modules:
  0.0 79.4 jit_solution(12056251382986726764)
XLA Ops:
  0.0 0.0 copy-start
  0.0 3.4 %copy-done = f32[128,8,2048]{2,1,0:T(8,128)S(1)} copy-done((f32[128,8,2048]{2,1,0:T(8,128)S(1)}, f32[128,8,2048]{2,1,0:T(8,128)}, u32[]{:S(2)}) %copy-start) | copy-done | bytes 8388632
  3.4 0.0 copy-start.1
  3.4 2.2 %copy-done.1 = f32[1,512,2048]{2,1,0:T(8,128)S(1)} copy-done((f32[1,512,2048]{2,1,0:T(8,128)S(1)}, f32[1,512,2048]{2,1,0:T(8,128)}, u32[]{:S(2)}) %copy-start.1) | copy-done | bytes 4194328
  5.6 0.0 copy-start.2
  5.6 1.0 %copy-done.2 = bf16[256,1024]{1,0:T(8,128)(2,1)S(1)} copy-done((bf16[256,1024]{1,0:T(8,128)(2,1)S(1)}, bf16[256,1024]{1,0:T(8,128)(2,1)}, u32[]{:S(2)}) %copy-start.2) | copy-done | bytes 524312
  6.6 0.0 copy-start.3
  6.6 1.0 %copy-done.3 = bf16[256,1024]{1,0:T(8,128)(2,1)S(1)} copy-done((bf16[256,1024]{1,0:T(8,128)(2,1)S(1)}, bf16[256,1024]{1,0:T(8,128)(2,1)}, u32[]{:S(2)}) %copy-start.3) | copy-done | bytes 524312
  7.7 7.7 %spectra.1 = bf16[32,96,128]{2,1,0:T(8,128)(2,1)S(1)} custom-call(bf16[256,1024]{1,0:T(8,128)(2,1)S(1)} %copy-done.3, bf16[256,1024]{1,0:T(8,128)(2,1)S(1)} %copy-done.2, f32[512,2048]{1,0:T(8,128)S(1)} %bitcast.17, f32[512,2048]{1,0:T(8,128)S(1)} %bitcast.18, f32[1024,2048]{1,0:T(8,128)S(1)} %bitcast.13, f32[1024,2048]{1,0:T(8,128)S(1)} %bitcast.14, ...), custom_call_target="tpu_custom_call" | custom-call | tf_op jit(solution)/shard_map/spectra/pallas_call | solution.py:81
  15.4 0.0 copy-start.4
  15.4 22.5 %all_to_all.19 = bf16[32,96,128]{2,1,0:T(8,128)(2,1)S(1)} all-to-all(bf16[32,96,128]{2,1,0:T(8,128)(2,1)S(1)} %spectra.1), channel_id=1, replica_groups=mesh['z'=8,'yh'=2,'core'=2,'x'=4,'yl'=2] {'x','yl','yh','core'}, dimensions={0} | all-to-all | bytes 1572864 | tf_op jit(solution)/shard_map/all_to_all | solution.py:151
  37.9 20.3 %all_to_all.20 = bf16[8,128,128]{2,1,0:T(8,128)(2,1)S(1)} all-to-all(bf16[8,128,128]{2,1,0:T(8,128)(2,1)S(1)} %bitcast.22), channel_id=1, replica_groups=mesh['z'=8,'yh'=2,'core'=2,'x'=4,'yl'=2] {'z'}, dimensions={0} | all-to-all | bytes 524288 | tf_op jit(solution)/shard_map/all_to_all | solution.py:152
  58.2 0.8 %product.1 = f32[256,128]{1,0:T(8,128)S(1)} custom-call(bf16[1024,128]{1,0:T(8,128)(2,1)S(1)} %bitcast.20, bf16[3072,128]{1,0:T(8,128)(2,1)S(1)} %bitcast.19), custom_call_target="tpu_custom_call" | custom-call | tf_op jit(solution)/shard_map/product/pallas_call | solution.py:137
  59.1 18.5 %all_to_all.21 = f32[256,1,128]{2,1,0:T(1,128)S(1)} all-to-all(f32[256,1,128]{2,1,0:T(1,128)S(1)} %bitcast.21), channel_id=1, replica_groups=mesh['z'=8,'yh'=2,'core'=2,'x'=4,'yl'=2] {'z','yh','core','x','yl'}, dimensions={0} | all-to-all | bytes 262144 | tf_op jit(solution)/shard_map/all_to_all | solution.py:154
  77.6 0.1 reshape.33
  77.7 0.0 copy-done.4
  77.7 1.7 %fusion = f32[1,8,2048]{2,1,0:T(8,128)} fusion(f32[256,8]{1,0:T(8,128)S(1)} %reshape.33, f32[256,2048]{1,0:T(8,128)S(1)} %copy-done.4), kind=kOutput, calls=%fused_computation.1 | convolution fusion | flops 50348032 | bytes 2170880 | tf_op jit(solution)/shard_map/dot_general | solution.py:157
  (2 shorter events, 0.0 us)
Async XLA Ops:
  0.0 3.4 %copy-start = (f32[128,8,2048]{2,1,0:T(8,128)S(1)}, f32[128,8,2048]{2,1,0:T(8,128)}, u32[]{:S(2)}) copy-start(f32[128,8,2048]{2,1,0:T(8,128)} %param.6) | copy-start | bytes 25165828
  3.4 2.2 %copy-start.1 = (f32[1,512,2048]{2,1,0:T(8,128)S(1)}, f32[1,512,2048]{2,1,0:T(8,128)}, u32[]{:S(2)}) copy-start(f32[1,512,2048]{2,1,0:T(8,128)} %param.5) | copy-start | bytes 12582916
  5.6 1.0 %copy-start.2 = (bf16[256,1024]{1,0:T(8,128)(2,1)S(1)}, bf16[256,1024]{1,0:T(8,128)(2,1)}, u32[]{:S(2)}) copy-start(bf16[256,1024]{1,0:T(8,128)(2,1)} %constant.11.clone.to_ref) | copy-start | bytes 1572868
  6.6 1.0 %copy-start.3 = (bf16[256,1024]{1,0:T(8,128)(2,1)S(1)}, bf16[256,1024]{1,0:T(8,128)(2,1)}, u32[]{:S(2)}) copy-start(bf16[256,1024]{1,0:T(8,128)(2,1)} %constant.10.clone.te_ref) | copy-start | bytes 1572868
  15.4 62.3 %copy-start.4 = (f32[256,2048]{1,0:T(8,128)S(1)}, f32[256,2048]{1,0:T(8,128)}, u32[]{:S(2)}) copy-start(f32[256,2048]{1,0:T(8,128)} %constant.12.clone) | copy-start | bytes 6291460

commit v2 on v1

v2 whole, which is shorter than its diff:
```python
import math

import jax
import jax.numpy as jnp
import ml_dtypes
import numpy as np
from jax import lax
from jax.experimental import pallas as pl
from jax.experimental.pallas import tpu as pltpu
from jax.sharding import Mesh, PartitionSpec as P

K = 4096
NT = 2048
NF = 128
F_LO = 256
HALF = NT // 2
TB = 256
ALL = ("z", "yh", "core", "x", "yl")
PLANE = ("x", "yl", "yh", "core")


def bins_of_plane():
    even = F_LO + 2 * np.arange(NF // 2)
    return np.concatenate([even, even + 1]).reshape(32, 4)


def table_rows(bins):
    phase = (bins[..., None] * np.arange(NT)) % NT * (2.0 * np.pi / NT)
    return np.stack([np.cos(phase), -np.sin(phase)], -2)


def split_bf16(x):
    hi = x.astype(np.float32).astype(ml_dtypes.bfloat16)
    lo = (x - hi.astype(np.float64)).astype(np.float32).astype(ml_dtypes.bfloat16)
    return hi, lo


def spectra_kernel(w_hbm, l_hbm, r_hbm, out_ref, w_ref, l_ref, r_ref, acc_ref, sems):
    copies = []

    def copy(src, dst):
        copies.append(pltpu.make_async_copy(src, dst, sems.at[len(copies)]))
        return copies[-1]

    stages = []
    for c in range(4):
        spans = [pl.ds(n * HALF + c * TB, TB) for n in range(2)]
        stages.append([copy(r_hbm.at[:, span], r_ref.at[:, span]) for span in spans])
        stages[-1].append(copy(w_hbm.at[:, spans[0]], w_ref.at[:, spans[0]]))
    for c in range(2):
        rows = pl.ds(c * 256, 256)
        stages.append([copy(l_hbm.at[rows], l_ref.at[rows])])
    for stage in stages:
        for one in stage:
            one.start()

    def times_table(x, w):
        hi = x.astype(jnp.bfloat16)
        lo = (x - hi.astype(jnp.float32)).astype(jnp.bfloat16)
        y = jnp.dot(hi, w, preferred_element_type=jnp.float32)
        z = jnp.dot(lo, w[:, :128], preferred_element_type=jnp.float32)
        return y[:, :128] + (y[:, 128:] + z)

    def put(half, block, values):
        pair = [(v * (1.0 / math.sqrt(NT))).T.reshape(16, 8, 128) for v in values]
        rows = slice(block * 16, block * 16 + 16)
        out_ref[half * 16 : half * 16 + 16, rows, :] = jnp.concatenate(pair, 1).astype(jnp.bfloat16)

    for c in range(4):
        for one in stages[c]:
            one.wait()
        a = r_ref[:, c * TB : c * TB + TB]
        b = r_ref[:, HALF + c * TB : HALF + c * TB + TB]
        for half in range(2):
            y = times_table(a - b if half else a + b, w_ref[half, c * TB : c * TB + TB, :])
            if c == 0:
                acc_ref[half] = y
            else:
                acc_ref[half] += y
    for half in range(2):
        for n in range(4):
            put(half, 2 + n, [acc_ref[half, pl.ds(2 * n + m, 128, stride=8), :] for m in range(2)])
    for c in range(2):
        for one in stages[4 + c]:
            one.wait()
        a = l_ref[c * 256 : c * 256 + 256, :HALF]
        b = l_ref[c * 256 : c * 256 + 256, HALF:]
        for half in range(2):
            y = times_table(a - b if half else a + b, w_ref[half])
            put(half, c, [y[:128], y[128:]])


def spectra(left, right, table):
    return pl.pallas_call(
        spectra_kernel,
        out_shape=jax.ShapeDtypeStruct((32, 96, 128), jnp.bfloat16),
        in_specs=[pl.BlockSpec(memory_space=pl.ANY)] * 3,
        out_specs=pl.BlockSpec(memory_space=pltpu.VMEM),
        scratch_shapes=[
            pltpu.VMEM((2, HALF, 256), jnp.bfloat16),
            pltpu.VMEM((512, NT), jnp.float32),
            pltpu.VMEM((1024, NT), jnp.float32),
            pltpu.VMEM((2, 1024, 128), jnp.float32),
            pltpu.SemaphoreType.DMA((14,)),
        ],
        compiler_params=pltpu.CompilerParams(vmem_limit_bytes=60 * 2**20),
        name="spectra",
    )(table, left, right)


def product_kernel(l_ref, g_ref, out_ref, lf_ref, rf_ref):
    lf_ref[...] = l_ref[...].astype(jnp.float32)
    for p in range(32):
        rf_ref[p * 64 : p * 64 + 64, :] = g_ref[p * 96 + 32 : p * 96 + 96, :].astype(jnp.float32)
    outs = []
    for f in range(4):
        left = [lf_ref[pl.ds(q * 8 + 2 * f + ri, 32, stride=32), :] for ri in range(2) for q in range(4)]
        lhs = jnp.concatenate(left, 1).astype(jnp.bfloat16)
        real_rows, imag_rows = [], []
        for yc in range(4):
            top, bottom = [], []
            for j in range(8):
                base = (j * 4 + yc) * 64 + 2 * f
                re = rf_ref[pl.ds(base, 8, stride=8), :]
                im = rf_ref[pl.ds(base + 1, 8, stride=8), :]
                top += [re, im]
                bottom += [-im, re]
            real_rows.append(jnp.concatenate(top, 0))
            imag_rows.append(jnp.concatenate(bottom, 0))
        rhs = jnp.concatenate(real_rows + imag_rows, 1).astype(jnp.bfloat16)
        outs.append(
            lax.dot_general(lhs, rhs, (((1,), (1,)), ((), ())), preferred_element_type=jnp.float32)
        )
    group = lax.broadcasted_iota(jnp.int32, (32, 128), 1) // 16
    for j in range(8):
        v = jnp.zeros((32, 128), jnp.float32)
        for f in range(4):
            moved = outs[f] if f == j else pltpu.roll(outs[f], (f - j) * 16 % 128, 1)
            v = jnp.where(group == f, moved, v)
        out_ref[pl.ds(j, 32, stride=8), :] = v


def product(left, gathered):
    return pl.pallas_call(
        product_kernel,
        out_shape=jax.ShapeDtypeStruct((256, 128), jnp.float32),
        scratch_shapes=[pltpu.VMEM((1024, 128), jnp.float32), pltpu.VMEM((2048, 128), jnp.float32)],
        compiler_params=pltpu.CompilerParams(vmem_limit_bytes=32 * 2**20),
        name="product",
    )(left, gathered)


def inverse_kernel(parts_ref, hi_ref, lo_ref, out_ref):
    total = parts_ref[0:32, :]
    for z in range(1, 8):
        total = total + parts_ref[z * 32 : z * 32 + 32, :]
    turned = jnp.concatenate([total, jnp.zeros((96, 128), jnp.float32)], 0).T
    halves = []
    for n in range(2):
        part = turned[n * 32 : n * 32 + 8, :]
        for g in range(1, 4):
            row = n * 32 + g * 8
            part = part + pltpu.roll(turned[row : row + 8, :], g * 32, 1)
        halves.append(part)
    spectrum = jnp.concatenate(halves, 1)
    hi = spectrum.astype(jnp.bfloat16)
    lo = (spectrum - hi.astype(jnp.float32)).astype(jnp.bfloat16)
    y = jnp.dot(hi, hi_ref[...], preferred_element_type=jnp.float32)
    y = y + jnp.dot(lo, hi_ref[...], preferred_element_type=jnp.float32)
    y = y + jnp.dot(hi, lo_ref[...], preferred_element_type=jnp.float32)
    out_ref[...] = y * (math.sqrt(2.0 / NF) / math.sqrt(K))


def inverse(parts, hi, lo):
    return pl.pallas_call(
        inverse_kernel,
        out_shape=jax.ShapeDtypeStruct((8, NT), jnp.float32),
        compiler_params=pltpu.CompilerParams(vmem_limit_bytes=32 * 2**20),
        name="inverse",
    )(parts, hi, lo)


def shards(left_traces, right_traces):
    table = table_rows(bins_of_plane())
    forward = table[..., :HALF].reshape(2, 128, HALF)
    forward = np.stack([np.concatenate(split_bf16(one.T), 1) for one in forward])
    backward = table.reshape(8, 4, 8, NT).transpose(2, 1, 0, 3).reshape(256, NT)
    sent = spectra(left_traces.reshape(512, NT), right_traces.reshape(1024, NT), forward)
    here = lax.all_to_all(sent, PLANE, 0, 0, tiled=True)
    left = lax.all_to_all(here[:, :32, :].reshape(8, 128, 128), "z", 0, 0, tiled=True)
    part = product(left.reshape(1024, 128), here.reshape(3072, 128))
    parts = lax.all_to_all(part, ALL, 0, 0, tiled=True)
    return inverse(parts, *split_bf16(backward)).reshape(1, 8, NT)


def solution(mesh):
    finer = Mesh(mesh.devices.reshape(8, 2, 2, 4, 2), ALL)
    placed = P(("z", "yh", "core"), ("x", "yl"), None)
    return jax.shard_map(
        shards, mesh=finer, in_specs=(placed, placed), out_specs=placed, check_vma=False
    )
```

time: 79.8 us -> 71.4 us (0.89)
  local copies, waits for them, and re-layouts: 7.77 us -> 0.03 us
  matrix products: 1.74 us -> 0 us
  Pallas kernels: 8.53 us -> 9.69 us
    unnamed x10 -> x4, local copies, waits for them, and re-layouts: 7.66 us -> 0.01 us
    dot_general x1 -> x0, matrix products: 1.74 us -> none  [shards(): lax.dot_general(spectrum, inverse, (((0,), (0,)), ((), ())), precision=la...]
    pallas_call x1 -> x2, Pallas kernels: 7.73 us -> 8.89 us  [the longest x1 7.61 us: spectra(): pl.pallas_call(spectra_kernel, out_shape=jax.ShapeDtypeStruct((32, 96, 12...]
where the time goes in v2:
time: 71.4 us; the launch traced here: 71.2 us
  blocking collectives  61.4 us (86%)
  Pallas kernels  9.69 us (14%)
    all_to_all x1, blocking collectives, shards(): here = lax.all_to_all(sent, PLANE, 0, 0, tiled=True)  22.6 us
    all_to_all x1, blocking collectives, shards(): lax.all_to_all(here[:, :32, :].reshape(8, 128, 128), 'z', 0, 0, tiled=True)  20.3 us
    all_to_all x1, blocking collectives, shards(): parts = lax.all_to_all(part, ALL, 0, 0, tiled=True)  18.5 us
    pallas_call x1, Pallas kernels, spectra(): pl.pallas_call(spectra_kernel, out_shape=jax.ShapeDtypeStruct((32, 96, 12...  7.61 us

profile of v2, /device:TPU:1, one launch (start us, length us, event | category | flops | bytes accessed | tf_op | source)
XLA Modules:
  0.0 71.2 jit_solution(6993167959213940667)
XLA Ops:
  0.0 0.0 copy-start
  0.0 0.0 copy-start.1
  0.0 7.6 %spectra.1 = bf16[32,96,128]{2,1,0:T(8,128)(2,1)} custom-call(bf16[2,1024,256]{2,1,0:T(8,128)(2,1)} %constant.6.clone.w_hbm, f32[512,2048]{1,0:T(8,128)} %bitcast.15, f32[1024,2048]{1,0:T(8,128)} %bitcast.14), custom_call_target="tpu_custom_call" | custom-call | tf_op jit(solution)/shard_map/spectra/pallas_call | solution.py:94
  7.6 22.6 %all_to_all.21 = bf16[32,96,128]{2,1,0:T(8,128)(2,1)S(1)} all-to-all(bf16[32,96,128]{2,1,0:T(8,128)(2,1)} %spectra.1), channel_id=1, replica_groups=mesh['z'=8,'yh'=2,'core'=2,'x'=4,'yl'=2] {'x','yl','yh','core'}, dimensions={0} | all-to-all | bytes 1572864 | tf_op jit(solution)/shard_map/all_to_all | solution.py:189
  30.2 20.3 %all_to_all.22 = bf16[8,128,128]{2,1,0:T(8,128)(2,1)S(1)} all-to-all(bf16[8,128,128]{2,1,0:T(8,128)(2,1)S(1)} %bitcast.16), channel_id=1, replica_groups=mesh['z'=8,'yh'=2,'core'=2,'x'=4,'yl'=2] {'z'}, dimensions={0} | all-to-all | bytes 524288 | tf_op jit(solution)/shard_map/all_to_all | solution.py:190
  50.6 0.8 %product.1 = f32[256,128]{1,0:T(8,128)S(1)} custom-call(bf16[1024,128]{1,0:T(8,128)(2,1)S(1)} %bitcast.11, bf16[3072,128]{1,0:T(8,128)(2,1)S(1)} %bitcast.10), custom_call_target="tpu_custom_call" | custom-call | tf_op jit(solution)/shard_map/product/pallas_call | solution.py:144
  51.4 18.5 %all_to_all.23 = f32[256,1,128]{2,1,0:T(1,128)S(1)} all-to-all(f32[256,1,128]{2,1,0:T(1,128)S(1)} %bitcast.13), channel_id=1, replica_groups=mesh['z'=8,'yh'=2,'core'=2,'x'=4,'yl'=2] {'z','yh','core','x','yl'}, dimensions={0} | all-to-all | bytes 262144 | tf_op jit(solution)/shard_map/all_to_all | solution.py:192
  69.9 0.0 copy-done
  69.9 0.0 copy-done.1
  69.9 1.3 %inverse.1 = f32[8,2048]{1,0:T(8,128)} custom-call(f32[256,128]{1,0:T(8,128)S(1)} %bitcast.12, bf16[256,2048]{1,0:T(8,128)(2,1)S(1)} %copy-done.1, bf16[256,2048]{1,0:T(8,128)(2,1)S(1)} %copy-done), custom_call_target="tpu_custom_call" | custom-call | tf_op jit(solution)/shard_map/inverse/pallas_call | solution.py:175
  (1 shorter events, 0.0 us)
Async XLA Ops:
  0.0 69.9 %copy-start = (bf16[256,2048]{1,0:T(8,128)(2,1)S(1)}, bf16[256,2048]{1,0:T(8,128)(2,1)}, u32[]{:S(2)}) copy-start(bf16[256,2048]{1,0:T(8,128)(2,1)} %constant.8.clone.lo_ref) | copy-start | bytes 3145732
  0.0 69.9 %copy-start.1 = (bf16[256,2048]{1,0:T(8,128)(2,1)S(1)}, bf16[256,2048]{1,0:T(8,128)(2,1)}, u32[]{:S(2)}) copy-start(bf16[256,2048]{1,0:T(8,128)(2,1)} %constant.7.clone.hi_ref) | copy-start | bytes 3145732

commit v3 on v2

v3 whole, which is shorter than its diff:
```python
import math

import jax
import jax.numpy as jnp
import ml_dtypes
import numpy as np
from jax import lax
from jax.experimental import pallas as pl
from jax.experimental.pallas import tpu as pltpu
from jax.sharding import Mesh, PartitionSpec as P

K = 4096
NT = 2048
NF = 128
F_LO = 256
HALF = NT // 2
TB = 256
AXES = ("za", "zb", "zc", "yh", "core", "xa", "xb", "yl")
Z = ("zb", "za", "zc")
PLANE = ("xb", "xa", "yl", "yh")


def bins_of_plane():
    even = F_LO + 2 * np.arange(NF // 2)
    return np.concatenate([even, even + 1]).reshape(16, 8)


def table_rows(bins):
    phase = (bins[..., None] * np.arange(NT)) % NT * (2.0 * np.pi / NT)
    return np.stack([np.cos(phase), -np.sin(phase)], -2)


def split_bf16(x):
    hi = x.astype(np.float32).astype(ml_dtypes.bfloat16)
    lo = (x - hi.astype(np.float64)).astype(np.float32).astype(ml_dtypes.bfloat16)
    return hi, lo


def spectra_kernel(w_hbm, l_hbm, r_hbm, out_ref, w_ref, l_ref, r_ref, acc_ref, sems):
    waits = []

    def fetch(src, dst, pieces):
        sem = sems.at[len(waits)]
        rows = src.shape[0] // pieces
        for n in range(pieces):
            part = pl.ds(n * rows, rows)
            pltpu.make_async_copy(src.at[part], dst.at[part], sem).start()
        waits.append(pltpu.make_async_copy(src, dst, sem))

    for c in range(4):
        spans = [pl.ds(n * HALF + c * TB, TB) for n in range(2)]
        fetch(w_hbm.at[:, spans[0]], w_ref.at[:, spans[0]], 1)
        for span in spans:
            fetch(r_hbm.at[:, span], r_ref.at[:, span], 8)
    fetch(l_hbm, l_ref, 16)

    def times_table(x, w):
        hi = x.astype(jnp.bfloat16)
        lo = (x - hi.astype(jnp.float32)).astype(jnp.bfloat16)
        y = jnp.dot(hi, w, preferred_element_type=jnp.float32)
        z = jnp.dot(lo, w[:, :128], preferred_element_type=jnp.float32)
        return y[:, :128] + (y[:, 128:] + z)

    def put(half, block, v):
        v = (v * (1.0 / math.sqrt(NT))).T.reshape(8, 16, 128)
        out_ref[half * 8 : half * 8 + 8, block * 16 : block * 16 + 16, :] = v.astype(jnp.bfloat16)

    for c in range(4):
        for one in waits[3 * c : 3 * c + 3]:
            one.wait()
        a = r_ref[:, c * TB : c * TB + TB]
        b = r_ref[:, HALF + c * TB : HALF + c * TB + TB]
        for half in range(2):
            y = times_table(a - b if half else a + b, w_ref[half, c * TB : c * TB + TB, :])
            if c == 0:
                acc_ref[half] = y
            else:
                acc_ref[half] += y
    for half in range(2):
        for r in range(8):
            put(half, 4 + r, acc_ref[half, pl.ds(r, 128, stride=8), :])
    waits[12].wait()
    a, b = l_ref[:, :HALF], l_ref[:, HALF:]
    for half in range(2):
        y = times_table(a - b if half else a + b, w_ref[half])
        for q in range(4):
            put(half, q, y[q * 128 : q * 128 + 128])


def spectra(left, right, table):
    return pl.pallas_call(
        spectra_kernel,
        out_shape=jax.ShapeDtypeStruct((16, 192, 128), jnp.bfloat16),
        in_specs=[pl.BlockSpec(memory_space=pl.ANY)] * 3,
        out_specs=pl.BlockSpec(memory_space=pltpu.VMEM),
        scratch_shapes=[
            pltpu.VMEM((2, HALF, 256), jnp.bfloat16),
            pltpu.VMEM((512, NT), jnp.float32),
            pltpu.VMEM((1024, NT), jnp.float32),
            pltpu.VMEM((2, 1024, 128), jnp.float32),
            pltpu.SemaphoreType.DMA((13,)),
        ],
        compiler_params=pltpu.CompilerParams(vmem_limit_bytes=60 * 2**20),
        name="spectra",
    )(table, left, right)


def product_kernel(l_ref, here_ref, there_ref, out_ref, lf_ref, rf_ref):
    own = lax.axis_index("core")
    lf_ref[...] = l_ref[...].astype(jnp.float32)
    for side, ref in enumerate((here_ref, there_ref)):
        for d in range(16):
            rows = slice(d * 128, d * 128 + 128)
            rf_ref[side, rows, :] = ref[d * 192 + 64 : d * 192 + 192, :].astype(jnp.float32)
    outs = []
    for f in range(8):
        left, real_rows, imag_rows = [[], []], [], []
        for side in range(2):
            core = own if side == 0 else 1 - own
            for yh in range(2):
                for ri in range(2):
                    row = yh * 32 + core * 16 + 2 * f + ri
                    shots = [lf_ref[pl.ds(row + n * 64, 8, stride=128), :] for n in range(2)]
                    left[ri].append(jnp.concatenate(shots, 0))
                top, bottom = [], []
                for j in range(8):
                    row = (j * 2 + yh) * 128 + 2 * f
                    re = rf_ref[side, pl.ds(row, 8, stride=16), :]
                    im = rf_ref[side, pl.ds(row + 1, 8, stride=16), :]
                    top += [re, im]
                    bottom += [-im, re]
                real_rows.append(jnp.concatenate(top, 0))
                imag_rows.append(jnp.concatenate(bottom, 0))
        lhs = jnp.concatenate(left[0] + left[1], 1).astype(jnp.bfloat16)
        rhs = jnp.concatenate(real_rows + imag_rows, 1).astype(jnp.bfloat16)
        outs.append(
            lax.dot_general(lhs, rhs, (((1,), (1,)), ((), ())), preferred_element_type=jnp.float32)
        )
    group = lax.broadcasted_iota(jnp.int32, (16, 128), 1) // 16
    for j in range(8):
        v = outs[j]
        for f in range(8):
            if f != j:
                v = jnp.where(group == f, pltpu.roll(outs[f], (f - j) * 16 % 128, 1), v)
        for yh in range(2):
            out_ref[pl.ds(j * 2 + yh, 8, stride=16), :] = v[yh * 8 : yh * 8 + 8]


def product(left, here, there):
    return pl.pallas_call(
        product_kernel,
        out_shape=jax.ShapeDtypeStruct((128, 128), jnp.float32),
        scratch_shapes=[pltpu.VMEM((1024, 128), jnp.float32), pltpu.VMEM((2, 2048, 128), jnp.float32)],
        compiler_params=pltpu.CompilerParams(vmem_limit_bytes=32 * 2**20),
        name="product",
    )(left, here, there)


def inverse_kernel(parts_ref, table_ref, out_ref):
    total = parts_ref[0:16, :]
    for z in range(1, 8):
        total = total + parts_ref[z * 16 : z * 16 + 16, :]
    turned = jnp.concatenate([total, jnp.zeros((112, 128), jnp.float32)], 0).T
    lane = lax.broadcasted_iota(jnp.int32, (8, 128), 1)
    sums = []
    for half in range(2):
        spectrum = jnp.zeros((8, 128), jnp.float32)
        for g in range(16):
            moved = pltpu.roll(turned[g * 8 : g * 8 + 8, :], (g - half) * 8 % 128, 1)
            spectrum = jnp.where(lane // 8 == g, moved, spectrum)
        hi = spectrum.astype(jnp.bfloat16)
        lo = (spectrum - hi.astype(jnp.float32)).astype(jnp.bfloat16)
        both = jnp.concatenate([hi.astype(jnp.float32), lo.astype(jnp.float32)], 0).astype(jnp.bfloat16)
        y = jnp.dot(both, table_ref[half, 0], preferred_element_type=jnp.float32)
        z = jnp.dot(both, table_ref[half, 1], preferred_element_type=jnp.float32)
        sums.append(y[:8] + (y[8:] + z[:8]))
    scale = math.sqrt(2.0 / NF) / math.sqrt(K)
    out_ref[:, :HALF] = (sums[0] + sums[1]) * scale
    out_ref[:, HALF:] = (sums[0] - sums[1]) * scale


def inverse(parts, table):
    return pl.pallas_call(
        inverse_kernel,
        out_shape=jax.ShapeDtypeStruct((8, NT), jnp.float32),
        compiler_params=pltpu.CompilerParams(vmem_limit_bytes=32 * 2**20),
        name="inverse",
    )(parts, table)


def shards(left_traces, right_traces):
    table = table_rows(bins_of_plane())[..., :HALF]
    forward = np.stack([np.concatenate(split_bf16(one.T), 1) for one in table.reshape(2, 128, HALF)])
    backward = table.reshape(2, 8, 16, HALF).transpose(0, 2, 1, 3).reshape(2, 128, HALF)
    backward = np.stack(split_bf16(backward), 1)
    sent = spectra(left_traces.reshape(512, NT), right_traces.reshape(1024, NT), forward)
    here = lax.all_to_all(sent, PLANE, 0, 0, tiled=True)
    there = lax.ppermute(here, "core", [(0, 1), (1, 0)])
    left = lax.all_to_all(here[:, :64, :].reshape(8, 128, 128), Z, 0, 0, tiled=True)
    part = product(left.reshape(1024, 128), here.reshape(3072, 128), there.reshape(3072, 128))
    parts = lax.all_to_all(part, Z + PLANE, 0, 0, tiled=True)
    return inverse(parts, backward).reshape(1, 8, NT)


def solution(mesh):
    finer = Mesh(mesh.devices.reshape((2,) * 8), AXES)
    placed = P(("za", "zb", "zc", "yh", "core"), ("xa", "xb", "yl"), None)
    return jax.shard_map(
        shards, mesh=finer, in_specs=(placed, placed), out_specs=placed, check_vma=False
    )
```

time: 71.4 us -> 68.5 us (0.959)
  blocking collectives: 61.4 us -> 56.5 us
  starting transfers between devices: 0 us -> 1.96 us
    all_to_all x2, blocking collectives: 38.9 us -> 35.4 us  [the longest x1 19.7 us: shards(): parts = lax.all_to_all(part, Z + PLANE, 0, 0, tiled=True)]
    ppermute x0 -> x1, starting transfers between devices: none -> 1.96 us  [shards(): there = lax.ppermute(here, 'core', [(0, 1), (1, 0)])]
    all_to_all x1, blocking collectives: 22.6 us -> 21.1 us  [shards(): here = lax.all_to_all(sent, PLANE, 0, 0, tiled=True)]
  transfers between devices with their start and end apart: 0 -> 1, of which waited for: 0 -> 0; matrix products, arithmetic and copies ran while one was open for 0% -> 0% of each run, Pallas kernels for 0% -> 0%
where the time goes in v3:
time: 68.5 us; the launch traced here: 68.3 us
  blocking collectives  56.5 us (82%)
  Pallas kernels  9.77 us (14%)
  starting transfers between devices  1.96 us (3%)
    all_to_all x1, blocking collectives, shards(): here = lax.all_to_all(sent, PLANE, 0, 0, tiled=True)  21.1 us
    all_to_all x1, blocking collectives, shards(): parts = lax.all_to_all(part, Z + PLANE, 0, 0, tiled=True)  19.7 us
    all_to_all x1, blocking collectives, shards(): lax.all_to_all(here[:, :64, :].reshape(8, 128, 128), Z, 0, 0, tiled=True)  15.7 us
    pallas_call x1, Pallas kernels, spectra(): pl.pallas_call(spectra_kernel, out_shape=jax.ShapeDtypeStruct((16, 192, 1...  7.35 us
    ppermute x1, starting transfers between devices, shards(): there = lax.ppermute(here, 'core', [(0, 1), (1, 0)])  1.96 us
    pallas_call x1, Pallas kernels, product(): pl.pallas_call(product_kernel, out_shape=jax.ShapeDtypeStruct((128, 128),...  1.38 us
  transfers between devices with their start and end apart: 1, of which 0 were waited for; matrix products, arithmetic and copies ran while one was open for 0% of the time, Pallas kernels for 0%

profile of v3, /device:TPU:1, one launch (start us, length us, event | category | flops | bytes accessed | tf_op | source)
XLA Modules:
  0.0 68.3 jit_solution(7059068145617556145)
XLA Ops:
  0.0 0.0 copy-start
  0.0 7.3 %spectra.1 = bf16[16,192,128]{2,1,0:T(8,128)(2,1)} custom-call(bf16[2,1024,256]{2,1,0:T(8,128)(2,1)} %constant.4.clone.w_hbm, f32[512,2048]{1,0:T(8,128)} %bitcast.17, f32[1024,2048]{1,0:T(8,128)} %bitcast.16), custom_call_target="tpu_custom_call" | custom-call | tf_op jit(solution)/shard_map/spectra/pallas_call | solution.py:91
  7.4 21.1 %all_to_all.21 = bf16[16,192,128]{2,1,0:T(8,128)(2,1)S(1)} all-to-all(bf16[16,192,128]{2,1,0:T(8,128)(2,1)} %spectra.1), channel_id=1, replica_groups=mesh['za'=2,'zb'=2,'zc'=2,'yh'=2,'core'=2,'xa'=2,'xb'=2,'yl'=2] {'xb','x..., dimensions={0} | all-to-all | bytes 1572864 | tf_op jit(solution)/shard_map/all_to_all | solution.py:197
  28.4 2.0 %collective-permute-start = (bf16[16,192,128]{2,1,0:T(8,128)(2,1)S(1)}, bf16[16,192,128]{2,1,0:T(8,128)(2,1)S(1)}, u32[]{:S(2)}, u32[]{:S(2)}) collective-permute-start(bf16[16,192,128]{2,1,0:T(8,128)(2,1)S(1)} %all_to_all.21), channel_id=1, source_target_pairs={{0,8},{8,0},{1,9},{9,1},{2,10},{10,2},{3,11},{11,3},{4,12},{12,4},... | collective-permute-start | bytes 2359304 | tf_op jit(solution)/shard_map/ppermute | solution.py:198
  30.4 15.7 %all_to_all.22 = bf16[8,128,128]{2,1,0:T(8,128)(2,1)S(1)} all-to-all(bf16[8,128,128]{2,1,0:T(8,128)(2,1)S(1)} %bitcast.18), channel_id=1, replica_groups=mesh['za'=2,'zb'=2,'zc'=2,'yh'=2,'core'=2,'xa'=2,'xb'=2,'yl'=2] {'zb','z..., dimensions={0} | all-to-all | bytes 524288 | tf_op jit(solution)/shard_map/all_to_all | solution.py:199
  46.1 0.0 collective-permute-done
  46.1 1.4 %product.1 = f32[128,128]{1,0:T(8,128)S(1)} custom-call(bf16[1024,128]{1,0:T(8,128)(2,1)S(1)} %bitcast.12, bf16[3072,128]{1,0:T(8,128)(2,1)S(1)} %bitcast.11, bf16[3072,128]{1,0:T(8,128)(2,1)S(1)} %bitcast.13), custom_call_target="tpu_custom_call" | custom-call | tf_op jit(solution)/shard_map/product/pallas_call | solution.py:150
  47.5 19.7 %all_to_all.23 = f32[128,1,128]{2,1,0:T(1,128)S(1)} all-to-all(f32[128,1,128]{2,1,0:T(1,128)S(1)} %bitcast.15), channel_id=1, replica_groups=mesh['za'=2,'zb'=2,'zc'=2,'yh'=2,'core'=2,'xa'=2,'xb'=2,'yl'=2] {'zb','z..., dimensions={0} | all-to-all | bytes 131072 | tf_op jit(solution)/shard_map/all_to_all | solution.py:201
  67.2 0.0 copy-done
  67.2 1.0 %inverse.1 = f32[8,2048]{1,0:T(8,128)} custom-call(f32[128,128]{1,0:T(8,128)S(1)} %bitcast.14, bf16[2,2,128,1024]{3,2,1,0:T(8,128)(2,1)S(1)} %copy-done), custom_call_target="tpu_custom_call" | custom-call | tf_op jit(solution)/shard_map/inverse/pallas_call | solution.py:183
  (1 shorter events, 0.0 us)
Async XLA Ops:
  0.0 67.2 %copy-start = (bf16[2,2,128,1024]{3,2,1,0:T(8,128)(2,1)S(1)}, bf16[2,2,128,1024]{3,2,1,0:T(8,128)(2,1)}, u32[]{:S(2)}) copy-start(bf16[2,2,128,1024]{3,2,1,0:T(8,128)(2,1)} %constant.5.clone.table_ref) | copy-start | bytes 3145732
  28.4 17.7 %collective-permute-start = (bf16[16,192,128]{2,1,0:T(8,128)(2,1)S(1)}, bf16[16,192,128]{2,1,0:T(8,128)(2,1)S(1)}, u32[]{:S(2)}, u32[]{:S(2)}) collective-permute-start(bf16[16,192,128]{2,1,0:T(8,128)(2,1)S(1)} %all_to_all.21), channel_id=1, source_target_pairs={{0,8},{8,0},{1,9},{9,1},{2,10},{10,2},{3,11},{11,3},{4,12},{12,4},... | collective-permute-start | bytes 2359304 | tf_op jit(solution)/shard_map/ppermute | solution.py:198

commit v4 on v3

--- a/solution.py
+++ b/solution.py
@@ -16,8 +16,8 @@
 HALF = NT // 2
 TB = 256
 AXES = ("za", "zb", "zc", "yh", "core", "xa", "xb", "yl")
-Z = ("zb", "za", "zc")
-PLANE = ("xb", "xa", "yl", "yh")
+Z = ("zb", "zc", "za")
+PLANE = ("xb", "yl", "xa", "yh")
 
 
 def bins_of_plane():
@@ -78,7 +78,10 @@
                 acc_ref[half] += y
     for half in range(2):
         for r in range(8):
-            put(half, 4 + r, acc_ref[half, pl.ds(r, 128, stride=8), :])
+            rows = pl.ds(r, 128, stride=8)
+            acc_ref[half, rows, :] = (acc_ref[half, rows, :] * (1.0 / math.sqrt(NT))).T
+        turned = acc_ref[half].reshape(8, 128, 128).astype(jnp.bfloat16)
+        out_ref[half * 8 : half * 8 + 8, 64:192, :] = turned
     waits[12].wait()
     a, b = l_ref[:, :HALF], l_ref[:, HALF:]
     for half in range(2):
@@ -90,7 +93,7 @@
 def spectra(left, right, table):
     return pl.pallas_call(
         spectra_kernel,
-        out_shape=jax.ShapeDtypeStruct((16, 192, 128), jnp.bfloat16),
+        out_shape=pltpu.VMEM((16, 192, 128), jnp.bfloat16),
         in_specs=[pl.BlockSpec(memory_space=pl.ANY)] * 3,
         out_specs=pl.BlockSpec(memory_space=pltpu.VMEM),
         scratch_shapes=[
@@ -100,48 +103,42 @@
             pltpu.VMEM((2, 1024, 128), jnp.float32),
             pltpu.SemaphoreType.DMA((13,)),
         ],
-        compiler_params=pltpu.CompilerParams(vmem_limit_bytes=60 * 2**20),
+        compiler_params=pltpu.CompilerParams(vmem_limit_bytes=32 * 2**20),
         name="spectra",
-    )(table, left, right)
-
-
-def product_kernel(l_ref, here_ref, there_ref, out_ref, lf_ref, rf_ref):
+    )(*(pltpu.with_memory_space_constraint(x, pltpu.HBM) for x in (table, left, right)))
+
+
+def product_kernel(l_ref, here_ref, there_ref, out_ref, lf_ref):
     own = lax.axis_index("core")
     lf_ref[...] = l_ref[...].astype(jnp.float32)
-    for side, ref in enumerate((here_ref, there_ref)):
-        for d in range(16):
-            rows = slice(d * 128, d * 128 + 128)
-            rf_ref[side, rows, :] = ref[d * 192 + 64 : d * 192 + 192, :].astype(jnp.float32)
+    lane = lax.broadcasted_iota(jnp.int32, (16, 128), 1)
     outs = []
     for f in range(8):
-        left, real_rows, imag_rows = [[], []], [], []
-        for side in range(2):
+        left, right = [[], []], []
+        for side, ref in enumerate((here_ref, there_ref)):
             core = own if side == 0 else 1 - own
             for yh in range(2):
                 for ri in range(2):
                     row = yh * 32 + core * 16 + 2 * f + ri
                     shots = [lf_ref[pl.ds(row + n * 64, 8, stride=128), :] for n in range(2)]
                     left[ri].append(jnp.concatenate(shots, 0))
-                top, bottom = [], []
-                for j in range(8):
-                    row = (j * 2 + yh) * 128 + 2 * f
-                    re = rf_ref[side, pl.ds(row, 8, stride=16), :]
-                    im = rf_ref[side, pl.ds(row + 1, 8, stride=16), :]
-                    top += [re, im]
-                    bottom += [-im, re]
-                real_rows.append(jnp.concatenate(top, 0))
-                imag_rows.append(jnp.concatenate(bottom, 0))
-        lhs = jnp.concatenate(left[0] + left[1], 1).astype(jnp.bfloat16)
-        rhs = jnp.concatenate(real_rows + imag_rows, 1).astype(jnp.bfloat16)
-        outs.append(
-            lax.dot_general(lhs, rhs, (((1,), (1,)), ((), ())), preferred_element_type=jnp.float32)
+                starts = [(j * 2 + yh) * 192 + 64 + f * 16 for j in range(8)]
+                right.append(jnp.concatenate([ref[row : row + 16, :] for row in starts], 0))
+        lhs = jnp.concatenate([jnp.concatenate(part, 1) for part in left], 0).astype(jnp.bfloat16)
+        y = lax.dot_general(
+            lhs,
+            jnp.concatenate(right, 1),
+            (((1,), (1,)), ((), ())),
+            preferred_element_type=jnp.float32,
         )
-    group = lax.broadcasted_iota(jnp.int32, (16, 128), 1) // 16
+        by_re, by_im = y[:16], y[16:]
+        turned = jnp.where(lane % 16 < 8, -pltpu.roll(by_im, 120, 1), pltpu.roll(by_im, 8, 1))
+        outs.append(by_re + turned)
     for j in range(8):
         v = outs[j]
         for f in range(8):
             if f != j:
-                v = jnp.where(group == f, pltpu.roll(outs[f], (f - j) * 16 % 128, 1), v)
+                v = jnp.where(lane // 16 == f, pltpu.roll(outs[f], (f - j) * 16 % 128, 1), v)
         for yh in range(2):
             out_ref[pl.ds(j * 2 + yh, 8, stride=16), :] = v[yh * 8 : yh * 8 + 8]
 
@@ -150,7 +147,7 @@
     return pl.pallas_call(
         product_kernel,
         out_shape=jax.ShapeDtypeStruct((128, 128), jnp.float32),
-        scratch_shapes=[pltpu.VMEM((1024, 128), jnp.float32), pltpu.VMEM((2, 2048, 128), jnp.float32)],
+        scratch_shapes=[pltpu.VMEM((1024, 128), jnp.float32)],
         compiler_params=pltpu.CompilerParams(vmem_limit_bytes=32 * 2**20),
         name="product",
     )(left, here, there)

time: 68.5 us -> 66.3 us (0.968)
  Pallas kernels: 9.77 us -> 8.26 us
    pallas_call x1, Pallas kernels: 7.35 us -> 6.49 us  [spectra(): pl.pallas_call(spectra_kernel, out_shape=pltpu.VMEM((16, 192, 128), jnp.b...]
where the time goes in v4:
time: 66.3 us; the launch traced here: 66.1 us
  blocking collectives  55.9 us (84%)
  Pallas kernels  8.26 us (12%)
  starting transfers between devices  1.84 us (3%)
    all_to_all x1, blocking collectives, shards(): here = lax.all_to_all(sent, PLANE, 0, 0, tiled=True)  21 us
    all_to_all x1, blocking collectives, shards(): parts = lax.all_to_all(part, Z + PLANE, 0, 0, tiled=True)  19.3 us
    all_to_all x1, blocking collectives, shards(): lax.all_to_all(here[:, :64, :].reshape(8, 128, 128), Z, 0, 0, tiled=True)  15.7 us
    pallas_call x1, Pallas kernels, spectra(): pl.pallas_call(spectra_kernel, out_shape=pltpu.VMEM((16, 192, 128), jnp.b...  6.49 us
    ppermute x1, starting transfers between devices, shards(): there = lax.ppermute(here, 'core', [(0, 1), (1, 0)])  1.84 us
  transfers between devices with their start and end apart: 1, of which 0 were waited for; matrix products, arithmetic and copies ran while one was open for 0% of the time, Pallas kernels for 0%

profile of v4, /device:TPU:1, one launch (start us, length us, event | category | flops | bytes accessed | tf_op | source)
XLA Modules:
  0.0 66.1 jit_solution(12538296903864544383)
XLA Ops:
  0.0 0.0 copy-start
  0.0 6.5 %spectra.1 = bf16[16,192,128]{2,1,0:T(8,128)(2,1)S(1)} custom-call(bf16[2,1024,256]{2,1,0:T(8,128)(2,1)} %constant.4.clone.w_hbm, f32[512,2048]{1,0:T(8,128)} %bitcast.17, f32[1024,2048]{1,0:T(8,128)} %bitcast.16), custom_call_target="tpu_custom_call" | custom-call | tf_op jit(solution)/shard_map/spectra/pallas_call | solution.py:94
  6.5 21.0 %all_to_all.21 = bf16[16,192,128]{2,1,0:T(8,128)(2,1)S(1)} all-to-all(bf16[16,192,128]{2,1,0:T(8,128)(2,1)S(1)} %spectra.1), channel_id=1, replica_groups=mesh['za'=2,'zb'=2,'zc'=2,'yh'=2,'core'=2,'xa'=2,'xb'=2,'yl'=2] {'xb','y..., dimensions={0} | all-to-all | bytes 1572864 | tf_op jit(solution)/shard_map/all_to_all | solution.py:194
  27.5 1.8 %collective-permute-start = (bf16[16,192,128]{2,1,0:T(8,128)(2,1)S(1)}, bf16[16,192,128]{2,1,0:T(8,128)(2,1)S(1)}, u32[]{:S(2)}, u32[]{:S(2)}) collective-permute-start(bf16[16,192,128]{2,1,0:T(8,128)(2,1)S(1)} %all_to_all.21), channel_id=1, source_target_pairs={{0,8},{8,0},{1,9},{9,1},{2,10},{10,2},{3,11},{11,3},{4,12},{12,4},... | collective-permute-start | bytes 2359304 | tf_op jit(solution)/shard_map/ppermute | solution.py:195
  29.3 15.7 %all_to_all.22 = bf16[8,128,128]{2,1,0:T(8,128)(2,1)S(1)} all-to-all(bf16[8,128,128]{2,1,0:T(8,128)(2,1)S(1)} %bitcast.18), channel_id=1, replica_groups=mesh['za'=2,'zb'=2,'zc'=2,'yh'=2,'core'=2,'xa'=2,'xb'=2,'yl'=2] {'zb','z..., dimensions={0} | all-to-all | bytes 524288 | tf_op jit(solution)/shard_map/all_to_all | solution.py:196
  45.0 0.0 collective-permute-done
  45.0 0.7 %product.1 = f32[128,128]{1,0:T(8,128)S(1)} custom-call(bf16[1024,128]{1,0:T(8,128)(2,1)S(1)} %bitcast.12, bf16[3072,128]{1,0:T(8,128)(2,1)S(1)} %bitcast.11, bf16[3072,128]{1,0:T(8,128)(2,1)S(1)} %bitcast.13), custom_call_target="tpu_custom_call" | custom-call | tf_op jit(solution)/shard_map/product/pallas_call | solution.py:147
  45.7 19.3 %all_to_all.23 = f32[128,1,128]{2,1,0:T(1,128)S(1)} all-to-all(f32[128,1,128]{2,1,0:T(1,128)S(1)} %bitcast.15), channel_id=1, replica_groups=mesh['za'=2,'zb'=2,'zc'=2,'yh'=2,'core'=2,'xa'=2,'xb'=2,'yl'=2] {'zb','z..., dimensions={0} | all-to-all | bytes 131072 | tf_op jit(solution)/shard_map/all_to_all | solution.py:198
  65.0 0.0 copy-done
  65.0 1.0 %inverse.1 = f32[8,2048]{1,0:T(8,128)} custom-call(f32[128,128]{1,0:T(8,128)S(1)} %bitcast.14, bf16[2,2,128,1024]{3,2,1,0:T(8,128)(2,1)S(1)} %copy-done), custom_call_target="tpu_custom_call" | custom-call | tf_op jit(solution)/shard_map/inverse/pallas_call | solution.py:180
  (1 shorter events, 0.0 us)
Async XLA Ops:
  0.0 65.0 %copy-start = (bf16[2,2,128,1024]{3,2,1,0:T(8,128)(2,1)S(1)}, bf16[2,2,128,1024]{3,2,1,0:T(8,128)(2,1)}, u32[]{:S(2)}) copy-start(bf16[2,2,128,1024]{3,2,1,0:T(8,128)(2,1)} %constant.5.clone.table_ref) | copy-start | bytes 3145732
  27.5 17.5 %collective-permute-start = (bf16[16,192,128]{2,1,0:T(8,128)(2,1)S(1)}, bf16[16,192,128]{2,1,0:T(8,128)(2,1)S(1)}, u32[]{:S(2)}, u32[]{:S(2)}) collective-permute-start(bf16[16,192,128]{2,1,0:T(8,128)(2,1)S(1)} %all_to_all.21), channel_id=1, source_target_pairs={{0,8},{8,0},{1,9},{9,1},{2,10},{10,2},{3,11},{11,3},{4,12},{12,4},... | collective-permute-start | bytes 2359304 | tf_op jit(solution)/shard_map/ppermute | solution.py:195

commit v5 on v4

--- a/solution.py
+++ b/solution.py
@@ -115,14 +115,14 @@
     outs = []
     for f in range(8):
         left, right = [[], []], []
-        for side, ref in enumerate((here_ref, there_ref)):
+        for side, (ref, height) in enumerate(((here_ref, 192), (there_ref, 128))):
             core = own if side == 0 else 1 - own
             for yh in range(2):
                 for ri in range(2):
                     row = yh * 32 + core * 16 + 2 * f + ri
                     shots = [lf_ref[pl.ds(row + n * 64, 8, stride=128), :] for n in range(2)]
                     left[ri].append(jnp.concatenate(shots, 0))
-                starts = [(j * 2 + yh) * 192 + 64 + f * 16 for j in range(8)]
+                starts = [(j * 2 + yh + 1) * height - 128 + f * 16 for j in range(8)]
                 right.append(jnp.concatenate([ref[row : row + 16, :] for row in starts], 0))
         lhs = jnp.concatenate([jnp.concatenate(part, 1) for part in left], 0).astype(jnp.bfloat16)
         y = lax.dot_general(
@@ -192,9 +192,9 @@
     backward = np.stack(split_bf16(backward), 1)
     sent = spectra(left_traces.reshape(512, NT), right_traces.reshape(1024, NT), forward)
     here = lax.all_to_all(sent, PLANE, 0, 0, tiled=True)
-    there = lax.ppermute(here, "core", [(0, 1), (1, 0)])
+    there = lax.ppermute(here[:, 64:, :], "core", [(0, 1), (1, 0)])
     left = lax.all_to_all(here[:, :64, :].reshape(8, 128, 128), Z, 0, 0, tiled=True)
-    part = product(left.reshape(1024, 128), here.reshape(3072, 128), there.reshape(3072, 128))
+    part = product(left.reshape(1024, 128), here.reshape(3072, 128), there.reshape(2048, 128))
     parts = lax.all_to_all(part, Z + PLANE, 0, 0, tiled=True)
     return inverse(parts, backward).reshape(1, 8, NT)
 

time: 66.3 us -> 66.4 us (level)
  no operation moved by 1% of the time
where the time goes in v5:
time: 66.4 us; the launch traced here: 66.2 us
  blocking collectives  55.9 us (84%)
  Pallas kernels  8.26 us (12%)
  starting transfers between devices  1.93 us (3%)
    all_to_all x1, blocking collectives, shards(): here = lax.all_to_all(sent, PLANE, 0, 0, tiled=True)  21 us
    all_to_all x1, blocking collectives, shards(): parts = lax.all_to_all(part, Z + PLANE, 0, 0, tiled=True)  19.4 us
    all_to_all x1, blocking collectives, shards(): lax.all_to_all(here[:, :64, :].reshape(8, 128, 128), Z, 0, 0, tiled=True)  15.6 us
    pallas_call x1, Pallas kernels, spectra(): pl.pallas_call(spectra_kernel, out_shape=pltpu.VMEM((16, 192, 128), jnp.b...  6.49 us
    ppermute x1, starting transfers between devices, shards(): there = lax.ppermute(here[:, 64:, :], 'core', [(0, 1), (1, 0)])  1.93 us
  transfers between devices with their start and end apart: 1, of which 0 were waited for; matrix products, arithmetic and copies ran while one was open for 0% of the time, Pallas kernels for 0%

profile of v5, /device:TPU:1, one launch (start us, length us, event | category | flops | bytes accessed | tf_op | source)
XLA Modules:
  0.0 66.2 jit_solution(5041035686090374735)
XLA Ops:
  0.0 0.0 copy-start
  0.0 6.5 %spectra.1 = bf16[16,192,128]{2,1,0:T(8,128)(2,1)S(1)} custom-call(bf16[2,1024,256]{2,1,0:T(8,128)(2,1)} %constant.4.clone.w_hbm, f32[512,2048]{1,0:T(8,128)} %bitcast.17, f32[1024,2048]{1,0:T(8,128)} %bitcast.16), custom_call_target="tpu_custom_call" | custom-call | tf_op jit(solution)/shard_map/spectra/pallas_call | solution.py:94
  6.5 21.0 %all_to_all.21 = bf16[16,192,128]{2,1,0:T(8,128)(2,1)S(1)} all-to-all(bf16[16,192,128]{2,1,0:T(8,128)(2,1)S(1)} %spectra.1), channel_id=1, replica_groups=mesh['za'=2,'zb'=2,'zc'=2,'yh'=2,'core'=2,'xa'=2,'xb'=2,'yl'=2] {'xb','y..., dimensions={0} | all-to-all | bytes 1572864 | tf_op jit(solution)/shard_map/all_to_all | solution.py:194
  27.5 1.9 %collective-permute-start = (bf16[16,128,128]{2,1,0:T(8,128)(2,1)S(1)}, bf16[16,128,128]{2,1,0:T(8,128)(2,1)S(1)}, u32[]{:S(2)}, u32[]{:S(2)}) collective-permute-start(bf16[16,128,128]{2,1,0:T(8,128)(2,1)S(1)} %slice.9), channel_id=1, source_target_pairs={{0,8},{8,0},{1,9},{9,1},{2,10},{10,2},{3,11},{11,3},{4,12},{12,4},... | collective-permute-start | bytes 1572872 | tf_op jit(solution)/shard_map/ppermute | solution.py:195
  29.5 15.6 %all_to_all.22 = bf16[8,128,128]{2,1,0:T(8,128)(2,1)S(1)} all-to-all(bf16[8,128,128]{2,1,0:T(8,128)(2,1)S(1)} %bitcast.18), channel_id=1, replica_groups=mesh['za'=2,'zb'=2,'zc'=2,'yh'=2,'core'=2,'xa'=2,'xb'=2,'yl'=2] {'zb','z..., dimensions={0} | all-to-all | bytes 524288 | tf_op jit(solution)/shard_map/all_to_all | solution.py:196
  45.1 0.0 collective-permute-done
  45.1 0.7 %product.1 = f32[128,128]{1,0:T(8,128)S(1)} custom-call(bf16[1024,128]{1,0:T(8,128)(2,1)S(1)} %bitcast.12, bf16[3072,128]{1,0:T(8,128)(2,1)S(1)} %bitcast.11, bf16[2048,128]{1,0:T(8,128)(2,1)S(1)} %bitcast.13), custom_call_target="tpu_custom_call" | custom-call | tf_op jit(solution)/shard_map/product/pallas_call | solution.py:147
  45.8 19.4 %all_to_all.23 = f32[128,1,128]{2,1,0:T(1,128)S(1)} all-to-all(f32[128,1,128]{2,1,0:T(1,128)S(1)} %bitcast.14), channel_id=1, replica_groups=mesh['za'=2,'zb'=2,'zc'=2,'yh'=2,'core'=2,'xa'=2,'xb'=2,'yl'=2] {'zb','z..., dimensions={0} | all-to-all | bytes 131072 | tf_op jit(solution)/shard_map/all_to_all | solution.py:198
  65.2 0.0 copy-done
  65.2 1.0 %inverse.1 = f32[8,2048]{1,0:T(8,128)} custom-call(f32[128,128]{1,0:T(8,128)S(1)} %bitcast.15, bf16[2,2,128,1024]{3,2,1,0:T(8,128)(2,1)S(1)} %copy-done), custom_call_target="tpu_custom_call" | custom-call | tf_op jit(solution)/shard_map/inverse/pallas_call | solution.py:180
  (2 shorter events, 0.1 us)
Async XLA Ops:
  0.0 65.2 %copy-start = (bf16[2,2,128,1024]{3,2,1,0:T(8,128)(2,1)S(1)}, bf16[2,2,128,1024]{3,2,1,0:T(8,128)(2,1)}, u32[]{:S(2)}) copy-start(bf16[2,2,128,1024]{3,2,1,0:T(8,128)(2,1)} %constant.5.clone.table_ref) | copy-start | bytes 3145732
  27.5 17.6 %collective-permute-start = (bf16[16,128,128]{2,1,0:T(8,128)(2,1)S(1)}, bf16[16,128,128]{2,1,0:T(8,128)(2,1)S(1)}, u32[]{:S(2)}, u32[]{:S(2)}) collective-permute-start(bf16[16,128,128]{2,1,0:T(8,128)(2,1)S(1)} %slice.9), channel_id=1, source_target_pairs={{0,8},{8,0},{1,9},{9,1},{2,10},{10,2},{3,11},{11,3},{4,12},{12,4},... | collective-permute-start | bytes 1572872 | tf_op jit(solution)/shard_map/ppermute | solution.py:195
